TPU v7x, 512 devices: a whole 4x4x16 slice. The times are simulated.
512 devices in a mesh: dp: 8 (over y, core), fsdp: 16 (over z), tensor: 4 (over x).
Axes of the slice: x: 4, y: 4, z: 16, core: 2. Of those that a mesh axis runs over, the one named last changes fastest.
Arguments:
- weight: float32 [4096, 4096], P('fsdp', 'tensor'), may hold values from -0.000234375 to 0.000234375
- momentum: bfloat16 [8, 4096, 4096], P('dp', 'fsdp', 'tensor'), may hold values from -8 to 8
- grads: bfloat16 [8, 2, 4096, 4096], P('dp', None, 'fsdp', 'tensor'), may hold values from -8 to 8
- right_factor: float32 [64, 4096], P(None, 'tensor'), may hold values from -1 to 1
Outputs:
- new_weight: float32 [4096, 4096], P('fsdp', 'tensor')
- new_momentum: bfloat16 [8, 4096, 4096], P('dp', 'fsdp', 'tensor')
- new_right: float32 [64, 4096], P(None, 'tensor')
All inputs are finite; a program needn't handle non-finite values.
Results may differ from a plain program's by a relative error of at most 0.001.
Values sent between devices are 32-bit elements; how exact they have to be, the bound alone decides.
A program may use at most 64 MiB of HBM per device.

v0:
```python
import functools
import math

import jax
import jax.numpy as jnp
from jax import lax
from jax.sharding import PartitionSpec as P

ROWS = 4096
COLS = 4096


decay_part = 0.05
learn_rate = 0.02
epsilon = 1e-06


def copy_for_each(x, axis):
    devices = lax.axis_size(axis)
    return lax.all_to_all(jnp.broadcast_to(x[None], (devices, *x.shape)), axis, 0, 0, tiled=True)


def of_everyone(x, axis):
    everything = copy_for_each(x, axis)
    return jnp.sum(everything, axis=0)


def in_blocks(x, dim, devices):
    shape = x.shape
    parts = x.reshape(*shape[:dim], devices, shape[dim] // devices, *shape[dim + 1 :])
    return jnp.moveaxis(parts, dim, 0)


def summed_on_arrival(x, axis, dim):
    devices = lax.axis_size(axis)
    parts = lax.all_to_all(in_blocks(x, dim, devices), axis, 0, 0, tiled=True)
    return jnp.sum(parts, axis=0)


def over_axes(x, axes):
    return functools.reduce(lax.psum, axes, x)


def gather_turned(arrays, axis, dims):
    turned = [jnp.moveaxis(a, dim, 0) for a, dim in zip(arrays, dims)]
    widths = [t[0].size for t in turned]
    both = jnp.concatenate([t.reshape(-1, w) for t, w in zip(turned, widths)], axis=1)
    result = lax.all_gather(both, axis, axis=0, tiled=True)
    parts = jnp.split(result, [sum(widths[:k]) for k in range(1, len(widths))], axis=1)
    return tuple(
        (
            jnp.moveaxis(b.reshape(-1, *t.shape[1:]), 0, dim)
            for b, t, dim in zip(parts, turned, dims)
        )
    )


def cholesky_step(factor, gram):
    lower = jnp.linalg.cholesky(gram)
    return jax.scipy.linalg.solve_triangular(lower, factor.T, lower=True).T


def local_gram(factor):
    return jnp.dot(
        factor.T, factor, precision=lax.Precision.HIGHEST, preferred_element_type=jnp.float32
    )


def orthonormal_rows(factor):
    for sweep in range(2):
        gram = of_everyone(local_gram(factor), "fsdp")
        factor = cholesky_step(factor, gram)
    return factor


def normalize(shared, sums):
    return shared / jnp.sqrt(sums + epsilon)[:, None]


def local(weight, momentum, grads, right_factor):
    replicas = lax.axis_size("dp")
    blended = momentum[0].astype(jnp.float32) + jnp.sum(grads[0].astype(jnp.float32), axis=0)
    partial_value = (
        jnp.dot(
            blended,
            right_factor.T,
            precision=lax.Precision.HIGHEST,
            preferred_element_type=jnp.float32,
        )
        / replicas
    )
    left = orthonormal_rows(of_everyone(partial_value, ("dp", "tensor")))
    partial_right = lax.dot_general(
        left,
        blended,
        (((0,), (0,)), ((), ())),
        precision=lax.Precision.HIGHEST,
        preferred_element_type=jnp.float32,
    )
    replica_share = summed_on_arrival(partial_right, "fsdp", 1)
    shared = of_everyone(replica_share, "dp") / replicas
    sums = over_axes(jnp.sum(shared * shared, axis=1), ("fsdp", "tensor"))
    right_share = normalize(shared, sums)
    replica_right, new_right = gather_turned((replica_share, right_share), "fsdp", (1, 1))
    projected = jnp.dot(
        left, replica_right, precision=lax.Precision.HIGHEST, preferred_element_type=jnp.float32
    )
    new_momentum = (blended - decay_part * projected).astype(jnp.bfloat16)[None]
    scale = learn_rate * math.sqrt(ROWS / COLS)
    new_weight = weight - scale * jnp.dot(
        left, new_right, precision=lax.Precision.HIGHEST, preferred_element_type=jnp.float32
    )
    return (new_weight, new_momentum, new_right)


def solution(mesh):
    placed = (
        P("fsdp", "tensor"),
        P("dp", "fsdp", "tensor"),
        P("dp", None, "fsdp", "tensor"),
        P(None, "tensor"),
    )
    return jax.shard_map(
        local,
        mesh=mesh,
        in_specs=placed,
        out_specs=(P("fsdp", "tensor"), P("dp", "fsdp", "tensor"), P(None, "tensor")),
        check_vma=False,
    )
```

profile of v0, /device:TPU:32, one launch (start us, length us, event | category | flops | bytes accessed | tf_op | source)
XLA Modules:
  0.0 240.6 jit_solution(13588295764593714555)
XLA Ops:
  0.7 1.6 convert_reduce_fusion
  2.3 1.1 convolution_multiply_fusion.2
  3.4 0.2 broadcast_in_dim.11
  3.6 35.4 %all_to_all.25 = f32[32,256,64]{1,2,0:T(8,128)S(1)} all-to-all(f32[32,256,64]{1,2,0:T(8,128)S(1)} %broadcast_in_dim.11), channel_id=1, replica_groups=mesh['dp'=8,'fsdp'=16,'tensor'=4] {'dp','tensor'}, dimensions={0} | all-to-all | bytes 4194304 | tf_op jit(solution)/shard_map/all_to_all | solution.py:20
  39.0 0.1 reduce_sum.64
  39.1 0.2 fusion.19
  39.4 0.3 reshape.26
  39.7 32.5 %all_to_all.26 = f32[16,1,4096]{2,1,0:T(1,128)S(1)} all-to-all(f32[16,1,4096]{2,1,0:T(1,128)S(1)} %reshape.26), channel_id=1, replica_groups=mesh['dp'=8,'fsdp'=16,'tensor'=4] {'fsdp'}, dimensions={0} | all-to-all | bytes 524288 | tf_op jit(solution)/shard_map/all_to_all | solution.py:20
  72.2 0.5 broadcast.48
  72.7 1.3 reduce.5
  74.1 0.2 reshape.27
  74.3 0.1 copy.25
  74.4 5.8 %cholesky.44 = f32[64,64]{1,0:T(8,128)S(1)} custom-call(f32[64,64]{1,0:T(8,128)S(1)} %fusion.16), custom_call_target="Cholesky" | custom-call | tf_op jit(solution)/shard_map/jit(cholesky)/cholesky | solution.py:59
  80.3 0.6 compare_reduce_fusion.1
  80.9 0.7 fusion.10
  81.6 4.9 %custom-call.6 = f32[1,64,64]{1,2,0:T(8,128)S(1)} custom-call(f32[1,64,64]{2,1,0:T(8,128)S(1)} %fusion.10), custom_call_target="InvertDiagBlocksLowerTriangular" | custom-call | tf_op jit(solution)/shard_map/jit(_solve_triangular)/triangular_solve | solution.py:60
  86.5 0.3 fusion.8
  86.8 0.2 fusion.20
  87.0 1.0 reshape.28
  88.1 6.1 %all-to-all-start.2 = ((f32[16,1,4096]{2,1,0:T(1,128)}), f32[16,1,4096]{2,1,0:T(1,128)S(1)}, u32[]{:S(2)}, u32[]{:S(2)}) async-start(f32[16,1,4096]{2,1,0:T(1,128)} %reshape.28), calls=%async_computation.2 | async-start | bytes 524288 | tf_op jit(solution)/shard_map/all_to_all | solution.py:20
  94.2 1.1 fusion.6
  95.3 1.6 copy.27
  96.8 14.9 %all-to-all-done.2 = f32[16,1,4096]{2,1,0:T(1,128)S(1)} async-done(((f32[16,1,4096]{2,1,0:T(1,128)}), f32[16,1,4096]{2,1,0:T(1,128)S(1)}, u32[]{:S(2)}, u32[]{:S(2)}) %all-to-all-start.2) | async-done | bytes 262176 | tf_op jit(solution)/shard_map/all_to_all | solution.py:20
  111.8 2.0 reduce.6
  113.8 1.1 reshape.29
  115.0 5.8 %cholesky.55 = f32[64,64]{1,0:T(8,128)S(1)} custom-call(f32[64,64]{1,0:T(8,128)S(1)} %fusion.14), custom_call_target="Cholesky" | custom-call | tf_op jit(solution)/shard_map/jit(cholesky)/cholesky | solution.py:59
  120.9 0.6 compare_reduce_fusion
  121.6 0.7 fusion.11
  122.2 4.9 %custom-call.7 = f32[1,64,64]{1,2,0:T(8,128)S(1)} custom-call(f32[1,64,64]{2,1,0:T(8,128)S(1)} %fusion.11), custom_call_target="InvertDiagBlocksLowerTriangular" | custom-call | tf_op jit(solution)/shard_map/jit(_solve_triangular)/triangular_solve | solution.py:60
  127.1 0.3 fusion.12
  127.4 1.7 convolution_bitcast_fusion
  129.1 0.3 reshape.30
  129.4 23.5 %all_to_all.27 = f32[16,1,4096]{2,1,0:T(1,128)S(1)} all-to-all(f32[16,1,4096]{2,1,0:T(1,128)S(1)} %reshape.30), channel_id=1, replica_groups=mesh['dp'=8,'fsdp'=16,'tensor'=4] {'fsdp'}, dimensions={0} | all-to-all | bytes 524288 | tf_op jit(solution)/shard_map/all_to_all | solution.py:36
  152.9 1.3 reduce.7
  154.2 0.2 reshape.31
  154.5 0.2 reshape.32
  154.6 10.0 %all_to_all.28 = f32[8,1,4096]{2,1,0:T(1,128)S(1)} all-to-all(f32[8,1,4096]{2,1,0:T(1,128)S(1)} %reshape.32), channel_id=1, replica_groups=mesh['dp'=8,'fsdp'=16,'tensor'=4] {'dp'}, dimensions={0} | all-to-all | bytes 262144 | tf_op jit(solution)/shard_map/all_to_all | solution.py:20
  164.6 1.0 reduce.8
  165.6 0.1 reshape.33
  165.7 0.1 multiply_reduce_fusion
  165.8 28.1 %psum.14 = f32[64]{0:T(128)S(1)} all-reduce(f32[64]{0:T(128)S(1)} %multiply_reduce_fusion), channel_id=1, replica_groups=mesh['dp'=8,'fsdp'=16,'tensor'=4] {'fsdp'}, use_global_device_ids=true, to_apply=%region_9.12 | all-reduce | flops 64 | bytes 512 | tf_op jit(solution)/shard_map/psum | solution.py:41
  193.9 9.2 %psum.15 = f32[64]{0:T(128)S(1)} all-reduce(f32[64]{0:T(128)S(1)} %psum.14), channel_id=1, replica_groups=mesh['dp'=8,'fsdp'=16,'tensor'=4] {'tensor'}, use_global_device_ids=true, to_apply=%region_10.13 | all-reduce | flops 64 | bytes 512 | tf_op jit(solution)/shard_map/psum | solution.py:41
  203.1 0.1 divide_bitcast_fusion
  203.3 32.0 %all_gather.3 = f32[1024,128]{1,0:T(8,128)S(1)} all-gather(f32[64,128]{1,0:T(8,128)S(1)} %copy.28), channel_id=1, replica_groups=mesh['dp'=8,'fsdp'=16,'tensor'=4] {'fsdp'}, dimensions={0}, use_global_device_ids=true | all-gather | bytes 557056 | tf_op jit(solution)/shard_map/all_gather | solution.py:48
  235.3 1.9 fusion.3
  237.2 0.2 slice_bitcast_fusion
  237.4 2.2 fusion.1
  239.7 0.9 copy.29
  (23 shorter events, 0.5 us)
Async XLA Ops:
  0.6 1.6 copy-start
  0.6 1.6 copy-start.1
  72.7 21.4 %copy-start.2 = (bf16[1,256,1024]{2,1,0:T(8,128)(2,1)S(1)}, bf16[1,256,1024]{2,1,0:T(8,128)(2,1)}, u32[]{:S(2)}) copy-start(bf16[1,256,1024]{2,1,0:T(8,128)(2,1)} %param.8) | copy-start | bytes 1572868
  88.1 23.7 %all-to-all-start.2 = ((f32[16,1,4096]{2,1,0:T(1,128)}), f32[16,1,4096]{2,1,0:T(1,128)S(1)}, u32[]{:S(2)}, u32[]{:S(2)}) async-start(f32[16,1,4096]{2,1,0:T(1,128)} %reshape.28), calls=%async_computation.2 | async-start | bytes 524288 | tf_op jit(solution)/shard_map/all_to_all | solution.py:20
  203.3 34.1 %copy-start.3 = (f32[256,1024]{1,0:T(8,128)S(1)}, f32[256,1024]{1,0:T(8,128)}, u32[]{:S(2)}) copy-start(f32[256,1024]{1,0:T(8,128)} %param.7) | copy-start | bytes 3145732
where the time goes:
time: 241 us
  blocking collectives  171 us (71%)
  other arithmetic  32.9 us (14%)
  waiting for transfers between devices  14.9 us (6%)
  matrix products  7.81 us (3%)
  local copies, waits for them, and re-layouts  7.26 us (3%)
  starting transfers between devices  6.09 us (3%)
    all_to_all x3, blocking collectives, copy_for_each(): lax.all_to_all(jnp.broadcast_to(x[None], (devices, *x.shape)), axis, 0, 0...  77.8 us
    psum x2, blocking collectives, over_axes(): return functools.reduce(lax.psum, axes, x)  37.3 us
    all_gather x1, blocking collectives, gather_turned(): result = lax.all_gather(both, axis, axis=0, tiled=True)  32 us
    all_to_all x1, blocking collectives, summed_on_arrival(): parts = lax.all_to_all(in_blocks(x, dim, devices), axis, 0, 0, tiled=True)  23.5 us
    all_to_all x1, waiting for transfers between devices, copy_for_each(): lax.all_to_all(jnp.broadcast_to(x[None], (devices, *x.shape)), axis, 0, 0...  14.9 us
    another operation x6, other arithmetic, cholesky_step(): lower = jnp.linalg.cholesky(gram)  13 us
    another operation x4, other arithmetic, cholesky_step(): return jax.scipy.linalg.solve_triangular(lower, factor.T, lower=True).T  11.1 us
    all_to_all x1, starting transfers between devices, copy_for_each(): lax.all_to_all(jnp.broadcast_to(x[None], (devices, *x.shape)), axis, 0, 0...  6.09 us
  transfers between devices with their start and end apart: 1, of which 1 were waited for; matrix products, arithmetic and copies ran while one was open for 1% of the time, Pallas kernels for 0%

commit v1 on v0

v1 whole, which is shorter than its diff:
```python
import functools
import math

import jax
import jax.numpy as jnp
from jax import lax
from jax.experimental import pallas as pl
from jax.experimental.pallas import tpu as pltpu
from jax.sharding import PartitionSpec as P

ROWS = 4096
COLS = 4096

decay_part = 0.05
learn_rate = 0.02
epsilon = 1e-06

MESH = pl.DeviceIdType.MESH
f32 = jnp.float32
bf16 = jnp.bfloat16
NN = (((1,), (0,)), ((), ()))
NT = (((1,), (1,)), ((), ()))


def split(x, n):
    parts = []
    for k in range(n):
        part = x.astype(bf16)
        parts.append(part)
        if k < n - 1:
            x = x - part.astype(f32)
    return parts


def dots(a, b, dims, order):
    total = None
    pairs = [(i, j) for i in range(len(a)) for j in range(len(b)) if i + j < order]
    for i, j in sorted(pairs, key=lambda t: -(t[0] + t[1])):
        term = lax.dot_general(a[i], b[j], dims, preferred_element_type=f32)
        total = term if total is None else total + term
    return total


def row_of(v, j):
    return jnp.broadcast_to(v[j : j + 1, :], (8, 128))


def lane_of(v, j):
    return jnp.broadcast_to(v[:, j : j + 1], (8, 128))


def eliminate(ref):
    sub = lax.broadcasted_iota(jnp.int32, (8, 128), 0)

    def body(kb, _):
        o = pl.multiple_of(kb * 8, 8)
        shift = lax.rem(128 - 8 * kb, 128)
        R = ref[pl.ds(o, 8), :]
        W = [R] + [ref[8 * i : 8 * i + 8, :] for i in range(1, 8)]
        D = [pltpu.roll(w, shift, 1) for w in W]
        C = [[lane_of(d, j) for j in range(8)] for d in D]
        Ls = [[None] * 8 for _ in range(8)]
        us = []
        for j in range(8):
            r = lax.rsqrt(row_of(C[0][j], j))
            for i in range(8):
                Ls[i][j] = C[i][j] * r
            u = row_of(R, j) * r
            us.append(u)
            R = R - Ls[0][j] * u
            for k in range(j + 1, 8):
                s = row_of(Ls[0][j], k)
                for i in range(8):
                    C[i][k] = C[i][k] - Ls[i][j] * s
        U = us[0]
        for j in range(1, 8):
            U = jnp.where(sub == j, us[j], U)
        for i in range(1, 8):
            w = W[i]
            for j in range(8):
                w = w - Ls[i][j] * us[j]
            ref[8 * i : 8 * i + 8, :] = jnp.where(i > kb, w, W[i])
        ref[pl.ds(o, 8), :] = U
        return 0

    lax.fori_loop(0, 8, body, 0)


def kernel(
    w_hbm, m_hbm, g_hbm, r_hbm, nw_hbm, nm_hbm, nr_hbm,
    w_v, m_v, g_v, r_v, bhi, blo,
    pc_send, pc_recv, p_send, p_recv, pk, qk,
    rr, rr_recv, rr_all, d_recv, sd, sd_recv, s_sub, s_all,
    gy, gx, hy, hx, aug, sq,
    nw_v, nm_v, nr_v,
    in_sem, out_sem, ssem, rsem,
):
    dp = lax.axis_index("dp")
    z = lax.axis_index("fsdp")
    x = lax.axis_index("tensor")
    y = dp // 2
    core = lax.rem(dp, 2)
    q = y * 4 + x

    loads = [
        pltpu.make_async_copy(m_hbm.at[0], m_v, in_sem.at[0]),
        pltpu.make_async_copy(g_hbm.at[0], g_v, in_sem.at[1]),
        pltpu.make_async_copy(r_hbm, r_v, in_sem.at[2]),
        pltpu.make_async_copy(w_hbm, w_v, in_sem.at[3]),
    ]
    for load in loads:
        load.start()

    mate = {"dp": y * 2 + 1 - core}
    plane = []
    for d in range(1, 16):
        o = lax.rem(q + d, 16)
        plane.append((o, {"dp": (o // 4) * 2 + core, "tensor": lax.rem(o, 4)}))
    column = []
    for d in range(1, 16):
        o = lax.rem(z + d, 16)
        column.append((o, {"fsdp": o}))
    replicas = []
    for d in range(1, 8):
        o = lax.rem(dp + d, 8)
        replicas.append((o, {"dp": o}))
    ys, xs = [], []
    for d in range(1, 4):
        o = lax.rem(y + d, 4)
        ys.append((o, {"dp": o * 2 + core}))
        o = lax.rem(x + d, 4)
        xs.append((o, {"tensor": o}))

    barrier = pltpu.get_barrier_semaphore()
    greeted = [mate] + [p for _, p in plane] + [p for _, p in column]
    for d in range(1, 4):
        greeted.append({"dp": lax.rem(y + d, 4) * 2 + 1 - core})
    for p in greeted:
        pl.semaphore_signal(barrier, inc=1, device_id=p, device_id_type=MESH)

    def send(phase, src, dst, peer):
        pltpu.make_async_remote_copy(
            src_ref=src, dst_ref=dst, send_sem=ssem.at[phase], recv_sem=rsem.at[phase],
            device_id=peer, device_id_type=MESH,
        ).start()

    def arrived(phase, like):
        pltpu.make_async_copy(like, like, rsem.at[phase]).wait()

    def sent(phase, like):
        pltpu.make_async_copy(like, like, ssem.at[phase]).wait()

    loads[0].wait()
    loads[1].wait()
    loads[2].wait()
    rp = split(r_v[...], 2)
    halves = []
    for h in range(2):
        rows = slice(128 * h, 128 * h + 128)
        b = m_v[rows, :].astype(f32) + (g_v[0, rows, :].astype(f32) + g_v[1, rows, :].astype(f32))
        bp = split(b, 2)
        bhi[rows, :] = bp[0]
        blo[rows, :] = bp[1]
        halves.append(dots(bp, rp, NT, 2) * 0.125)
    pc_send[...] = jnp.concatenate(halves, axis=1)

    pl.semaphore_wait(barrier, len(greeted))

    send(0, pc_send, pc_recv, mate)
    arrived(0, pc_recv)
    p_send[...] = (pc_send[...] + pc_recv[...]).reshape(16, 8, 128)
    p_recv[q] = p_send[q]
    for o, peer in plane:
        send(1, p_send.at[o], p_recv.at[q], peer)
    arrived(1, p_recv.at[pl.ds(0, 15)])
    mine = p_recv[0]
    for k in range(1, 16):
        mine = mine + p_recv[k]
    pk[q] = mine
    qk[z] = mine
    for o, peer in plane:
        send(2, pk.at[q], pk.at[q], peer)
    for o, peer in column:
        send(3, qk.at[z], qk.at[z], peer)

    arrived(2, pk.at[pl.ds(0, 15)])
    pt = pk[...].reshape(128, 128).T
    pt = jnp.concatenate([pt[:64], pt[64:]], axis=1)
    ptp = split(pt, 3)
    for c in range(4):
        cols = slice(256 * c, 256 * c + 256)
        part = dots(ptp, [bhi[:, cols], blo[:, cols]], NN, 3)
        for k in range(2):
            for h in range(2):
                rr[4 * c + 2 * k + h] = part[32 * h : 32 * h + 32, 128 * k : 128 * k + 128]
    for o, peer in column:
        send(4, rr.at[o], rr_recv.at[z], peer)
    rr_recv[z] = rr[z]
    for o, peer in replicas:
        send(5, rr.at[pl.ds(2 * o, 2)], d_recv.at[dp], peer)
    d_recv[dp] = rr[pl.ds(2 * dp, 2)]

    def share_gram(t, first, second, phase):
        tp = split(t, 3)
        g = dots(tp, tp, NT, 3)
        first[y] = jnp.concatenate([g[:32], g[32:]], axis=1)
        for o, peer in ys:
            send(phase, first.at[y], first.at[y], peer)

    def pass_gram(first, second, phase):
        arrived(phase, first.at[pl.ds(0, 3)])
        second[x] = (first[0] + first[1]) + (first[2] + first[3])
        for o, peer in xs:
            send(phase + 1, second.at[x], second.at[x], peer)

    def whole_gram(second, phase):
        arrived(phase + 1, second.at[pl.ds(0, 3)])
        g = (second[0] + second[1]) + (second[2] + second[3])
        return jnp.concatenate([g, pltpu.roll(g, 64, 1)], axis=0)

    lanes = lax.broadcasted_iota(jnp.int32, (64, 128), 1)
    ranks = lax.broadcasted_iota(jnp.int32, (64, 128), 0)

    arrived(3, qk.at[pl.ds(0, 15)])
    qt = qk[...].reshape(128, 128).T
    qt = jnp.concatenate([qt[:64], qt[64:]], axis=1)
    share_gram(qt, gy, gx, 6)
    pass_gram(gy, gx, 6)

    arrived(5, d_recv.at[pl.ds(0, 7)])
    total = d_recv[0]
    for k in range(1, 8):
        total = total + d_recv[k]
    total = total.reshape(64, 128)
    for k in range(16):
        sd[k] = total[4 * k : 4 * k + 4, :]
    for o, peer in column:
        send(10, sd.at[o], sd_recv.at[z], peer)
    sd_recv[z] = sd[z]

    g = whole_gram(gx, 6)
    aug[...] = jnp.where(lanes < 64, g, jnp.where(lanes == ranks + 64, 1.0, 0.0))
    eliminate(aug)
    first_inverse = aug[:, 64:]
    qt1 = dots(split(first_inverse, 3), split(qt, 3), NN, 3)
    share_gram(qt1, hy, hx, 8)

    arrived(4, rr_recv.at[pl.ds(0, 15)])
    total = rr_recv[0]
    for k in range(1, 16):
        total = total + rr_recv[k]
    rr_all[z] = total
    for o, peer in column:
        send(11, rr_all.at[z], rr_all.at[z], peer)

    arrived(10, sd_recv.at[pl.ds(0, 15)])
    total = sd_recv[0]
    for k in range(1, 16):
        total = total + sd_recv[k]
    s_sub[z] = total * 0.125
    for o, peer in column:
        send(12, s_sub.at[z], s_sub.at[z], peer)

    pass_gram(hy, hx, 8)
    g = whole_gram(hx, 8)
    aug[...] = jnp.where(lanes < 64, g, aug[...])
    eliminate(aug)
    inverse = split(aug[:, 64:], 3)
    leftt = dots(inverse, ptp, NN, 3)
    lp = split(leftt, 2)
    l0 = lp[0].astype(f32)
    l1 = lp[1].astype(f32)
    left3 = jnp.concatenate([l0, l0, l1], axis=0).T.astype(bf16)

    arrived(12, s_sub.at[pl.ds(0, 15)])
    for k in range(16):
        s_all[dp, 4 * k : 4 * k + 4, :] = s_sub[k]
    for o, peer in replicas:
        send(13, s_all.at[dp], s_all.at[dp], peer)

    arrived(11, rr_all.at[pl.ds(0, 15)])
    for c in range(4):
        cols = slice(256 * c, 256 * c + 256)
        raw = jnp.concatenate(
            [jnp.concatenate([rr_all[4 * c + h], rr_all[4 * c + 2 + h]], axis=1) for h in range(2)], axis=0
        )
        right = dots(inverse, split(raw, 3), NN, 3)
        r0, r1 = split(right, 2)
        right3 = jnp.concatenate([r0, r1, r0], axis=0)
        projected = lax.dot_general(left3, right3, NN, preferred_element_type=f32)
        b = m_v[:, cols].astype(f32) + (g_v[0, :, cols].astype(f32) + g_v[1, :, cols].astype(f32))
        nm_v[:, cols] = (b - decay_part * projected).astype(bf16)
    nm_out = pltpu.make_async_copy(nm_v, nm_hbm.at[0], out_sem.at[0])
    nm_out.start()

    arrived(13, s_all.at[pl.ds(0, 7)])
    sums = None
    for k in range(8):
        shared = dots(inverse, split(s_all[k], 3), NN, 3)
        nr_v[:, 128 * k : 128 * k + 128] = shared
        sums = shared * shared if sums is None else sums + shared * shared
    sums = jnp.sum(sums, axis=1, keepdims=True)
    small = lax.broadcasted_iota(jnp.int32, (8, 128), 1)
    tile = jnp.zeros((8, 128), f32)
    for i in range(8):
        tile = jnp.where(small == i, jnp.broadcast_to(sums[8 * i : 8 * i + 8], (8, 128)), tile)
    sq[x] = tile
    for o, peer in xs:
        send(14, sq.at[x], sq.at[x], peer)
    arrived(14, sq.at[pl.ds(0, 3)])
    tile = (sq[0] + sq[1]) + (sq[2] + sq[3])
    tile = 1.0 / jnp.sqrt(tile + epsilon)
    factor = jnp.concatenate([lane_of(tile, i) for i in range(8)], axis=0)
    for k in range(8):
        nr_v[:, 128 * k : 128 * k + 128] = nr_v[:, 128 * k : 128 * k + 128] * factor
    nr_out = pltpu.make_async_copy(nr_v, nr_hbm, out_sem.at[1])
    nr_out.start()
    loads[3].wait()
    scale = learn_rate * math.sqrt(ROWS / COLS)
    for c in range(4):
        cols = slice(256 * c, 256 * c + 256)
        r0, r1 = split(nr_v[:, cols], 2)
        right3 = jnp.concatenate([r0, r1, r0], axis=0)
        step = lax.dot_general(left3, right3, NN, preferred_element_type=f32)
        nw_v[:, cols] = w_v[:, cols] - scale * step
    nw_out = pltpu.make_async_copy(nw_v, nw_hbm, out_sem.at[2])
    nw_out.start()

    sent(0, pc_send)
    sent(1, p_send.at[pl.ds(0, 15)])
    sent(2, pk.at[pl.ds(0, 15)])
    sent(3, qk.at[pl.ds(0, 15)])
    sent(4, rr.at[pl.ds(0, 15)])
    sent(5, d_recv.at[pl.ds(0, 7)])
    sent(6, gy.at[pl.ds(0, 3)])
    sent(7, gx.at[pl.ds(0, 3)])
    sent(8, hy.at[pl.ds(0, 3)])
    sent(9, hx.at[pl.ds(0, 3)])
    sent(10, sd.at[pl.ds(0, 15)])
    sent(11, rr_all.at[pl.ds(0, 15)])
    sent(12, s_sub.at[pl.ds(0, 15)])
    sent(13, s_all.at[pl.ds(0, 7)])
    sent(14, sq.at[pl.ds(0, 3)])
    nm_out.wait()
    nr_out.wait()
    nw_out.wait()


def local(weight, momentum, grads, right_factor):
    rows, cols = weight.shape
    rank = right_factor.shape[0]
    vm = pltpu.VMEM
    return pl.pallas_call(
        kernel,
        out_shape=(
            jax.ShapeDtypeStruct(weight.shape, f32),
            jax.ShapeDtypeStruct(momentum.shape, bf16),
            jax.ShapeDtypeStruct(right_factor.shape, f32),
        ),
        in_specs=[pl.BlockSpec(memory_space=pl.ANY)] * 4,
        out_specs=[pl.BlockSpec(memory_space=pl.ANY)] * 3,
        scratch_shapes=[
            vm((rows, cols), f32),
            vm((rows, cols), bf16),
            vm((2, rows, cols), bf16),
            vm((rank, cols), f32),
            vm((rows, cols), bf16),
            vm((rows, cols), bf16),
            vm((128, 128), f32),
            vm((128, 128), f32),
            vm((16, 8, 128), f32),
            vm((16, 8, 128), f32),
            vm((16, 8, 128), f32),
            vm((16, 8, 128), f32),
            vm((16, 32, 128), f32),
            vm((16, 32, 128), f32),
            vm((16, 32, 128), f32),
            vm((8, 2, 32, 128), f32),
            vm((16, 4, 128), f32),
            vm((16, 4, 128), f32),
            vm((16, 4, 128), f32),
            vm((8, 64, 128), f32),
            vm((4, 32, 128), f32),
            vm((4, 32, 128), f32),
            vm((4, 32, 128), f32),
            vm((4, 32, 128), f32),
            vm((64, 128), f32),
            vm((4, 8, 128), f32),
            vm((rows, cols), f32),
            vm((rows, cols), bf16),
            vm((rank, cols), f32),
            pltpu.SemaphoreType.DMA((4,)),
            pltpu.SemaphoreType.DMA((3,)),
            pltpu.SemaphoreType.DMA((15,)),
            pltpu.SemaphoreType.DMA((15,)),
        ],
        compiler_params=pltpu.CompilerParams(
            collective_id=0, has_side_effects=True, vmem_limit_bytes=48 * 1024 * 1024
        ),
        name="dion_step",
    )(weight, momentum, grads, right_factor)


def solution(mesh):
    placed = (
        P("fsdp", "tensor"),
        P("dp", "fsdp", "tensor"),
        P("dp", None, "fsdp", "tensor"),
        P(None, "tensor"),
    )
    return jax.shard_map(
        local,
        mesh=mesh,
        in_specs=placed,
        out_specs=(P("fsdp", "tensor"), P("dp", "fsdp", "tensor"), P(None, "tensor")),
        check_vma=False,
    )
```

time: 241 us -> 76.3 us (0.32)
  the two profiles are of different devices: /device:TPU:32 before, /device:TPU:1 now
where the time goes in v1:
time: 76.3 us; the launch traced here: 76 us
  Pallas kernels  68.5 us (90%)
  local copies, waits for them, and re-layouts  6.9 us (9%)
    pallas_call x1, Pallas kernels, local(): pl.pallas_call(kernel, out_shape=(jax.ShapeDtypeStruct(weight.shape, f32)...  68.5 us
    unnamed x11, local copies, waits for them, and re-layouts  6.9 us

profile of v1, /device:TPU:1, one launch (start us, length us, event | category | flops | bytes accessed | tf_op | source)
XLA Modules:
  0.0 76.0 jit_solution(542495371781668597)
XLA Ops:
  0.6 0.0 copy-start
  0.6 1.2 %copy-done = f32[256,1024]{1,0:T(8,128)S(1)} copy-done((f32[256,1024]{1,0:T(8,128)S(1)}, f32[256,1024]{1,0:T(8,128)}, u32[]{:S(2)}) %copy-start) | copy-done | bytes 1048600
  1.9 0.0 copy-start.1
  1.9 1.2 %copy-done.1 = bf16[1,2,256,1024]{3,2,1,0:T(8,128)(2,1)S(1)} copy-done((bf16[1,2,256,1024]{3,2,1,0:T(8,128)(2,1)S(1)}, bf16[1,2,256,1024]{3,2,1,0:T(8,128)(2,1)}, u32[]{:S(2)}) %copy-start.1) | copy-done | bytes 1048600
  3.1 0.0 copy-start.2
  3.1 1.0 %copy-done.2 = bf16[1,256,1024]{2,1,0:T(8,128)(2,1)S(1)} copy-done((bf16[1,256,1024]{2,1,0:T(8,128)(2,1)S(1)}, bf16[1,256,1024]{2,1,0:T(8,128)(2,1)}, u32[]{:S(2)}) %copy-start.2) | copy-done | bytes 524312
  4.1 0.0 copy-start.3
  4.1 0.9 %copy-done.3 = f32[64,1024]{1,0:T(8,128)S(1)} copy-done((f32[64,1024]{1,0:T(8,128)S(1)}, f32[64,1024]{1,0:T(8,128)}, u32[]{:S(2)}) %copy-start.3) | copy-done | bytes 262168
  5.1 68.5 %dion_step.1 = (f32[256,1024]{1,0:T(8,128)S(1)}, bf16[1,256,1024]{2,1,0:T(8,128)(2,1)S(1)}, f32[64,1024]{1,0:T(8,128)S(1)}) custom-call(f32[256,1024]{1,0:T(8,128)S(1)} %copy-done, bf16[1,256,1024]{2,1,0:T(8,128)(2,1)S(1)} %copy-done.2, bf16[1,2,256,1024]{3,2,1,0:T(8,128)(2,1)S(1)} %copy-done.1, f32[64,1024]{1,0:T(8,128)S(1)} %copy-done.3), custom_call_target="tpu_custom_call" | custom-call | tf_op jit(solution)/shard_map/dion_step/pallas_call | solution.py:353
  73.6 1.0 %copy.10 = f32[256,1024]{1,0:T(8,128)} copy(f32[256,1024]{1,0:T(8,128)S(1)} %get-tuple-element.6) | data formatting | bytes 2097152
  74.5 0.8 %copy.11 = bf16[1,256,1024]{2,1,0:T(8,128)(2,1)} copy(bf16[1,256,1024]{2,1,0:T(8,128)(2,1)S(1)} %get-tuple-element.7) | data formatting | bytes 1048576
  75.3 0.7 copy.12
Async XLA Ops:
  0.6 1.2 %copy-start = (f32[256,1024]{1,0:T(8,128)S(1)}, f32[256,1024]{1,0:T(8,128)}, u32[]{:S(2)}) copy-start(f32[256,1024]{1,0:T(8,128)} %w_hbm.1) | copy-start | bytes 3145732
  1.9 1.2 %copy-start.1 = (bf16[1,2,256,1024]{3,2,1,0:T(8,128)(2,1)S(1)}, bf16[1,2,256,1024]{3,2,1,0:T(8,128)(2,1)}, u32[]{:S(2)}) copy-start(bf16[1,2,256,1024]{3,2,1,0:T(8,128)(2,1)} %g_hbm.1) | copy-start | bytes 3145732
  3.1 1.0 %copy-start.2 = (bf16[1,256,1024]{2,1,0:T(8,128)(2,1)S(1)}, bf16[1,256,1024]{2,1,0:T(8,128)(2,1)}, u32[]{:S(2)}) copy-start(bf16[1,256,1024]{2,1,0:T(8,128)(2,1)} %m_hbm.1) | copy-start | bytes 1572868
  4.1 0.9 %copy-start.3 = (f32[64,1024]{1,0:T(8,128)S(1)}, f32[64,1024]{1,0:T(8,128)}, u32[]{:S(2)}) copy-start(f32[64,1024]{1,0:T(8,128)} %r_hbm.1) | copy-start | bytes 786436

commit v2 on v1

--- a/solution.py
+++ b/solution.py
@@ -20,6 +20,8 @@
 bf16 = jnp.bfloat16
 NN = (((1,), (0,)), ((), ()))
 NT = (((1,), (1,)), ((), ()))
+
+AWAY = (0, 3, -3, 6, -6)
 
 
 def split(x, n):
@@ -90,7 +92,7 @@
     w_hbm, m_hbm, g_hbm, r_hbm, nw_hbm, nm_hbm, nr_hbm,
     w_v, m_v, g_v, r_v, bhi, blo,
     pc_send, pc_recv, p_send, p_recv, pk, qk,
-    rr, rr_recv, rr_all, d_recv, sd, sd_recv, s_sub, s_all,
+    rr, near, agg, far, rr_all, d_recv, sd, sd_recv, s_sub, s_all,
     gy, gx, hy, hx, aug, sq,
     nw_v, nm_v, nr_v,
     in_sem, out_sem, ssem, rsem,
@@ -111,7 +113,14 @@
     for load in loads:
         load.start()
 
+    def around(k):
+        return lax.rem(z + k + 16, 16)
+
     mate = {"dp": y * 2 + 1 - core}
+    across = [mate]
+    for d in range(1, 16):
+        o = lax.rem(q + d, 16)
+        across.append({"dp": (o // 4) * 2 + 1 - core, "tensor": lax.rem(o, 4)})
     plane = []
     for d in range(1, 16):
         o = lax.rem(q + d, 16)
@@ -132,9 +141,8 @@
         xs.append((o, {"tensor": o}))
 
     barrier = pltpu.get_barrier_semaphore()
-    greeted = [mate] + [p for _, p in plane] + [p for _, p in column]
-    for d in range(1, 4):
-        greeted.append({"dp": lax.rem(y + d, 4) * 2 + 1 - core})
+    everyone = [p for _, p in plane] + across
+    greeted = [p for _, p in column] + everyone
     for p in greeted:
         pl.semaphore_signal(barrier, inc=1, device_id=p, device_id_type=MESH)
 
@@ -193,9 +201,11 @@
         for k in range(2):
             for h in range(2):
                 rr[4 * c + 2 * k + h] = part[32 * h : 32 * h + 32, 128 * k : 128 * k + 128]
-    for o, peer in column:
-        send(4, rr.at[o], rr_recv.at[z], peer)
-    rr_recv[z] = rr[z]
+    for k in (3, 4, 1, 2, 0):
+        for side, step in enumerate((1, -1)):
+            o = around(step + AWAY[k])
+            send(4 if k > 2 else 15, rr.at[o], near.at[k, side], {"fsdp": around(step)})
+    send(16, rr.at[around(8)], far.at[0], {"fsdp": around(8)})
     for o, peer in replicas:
         send(5, rr.at[pl.ds(2 * o, 2)], d_recv.at[dp], peer)
     d_recv[dp] = rr[pl.ds(2 * dp, 2)]
@@ -225,6 +235,17 @@
     qt = qk[...].reshape(128, 128).T
     qt = jnp.concatenate([qt[:64], qt[64:]], axis=1)
     share_gram(qt, gy, gx, 6)
+
+    def forward(k):
+        agg[k - 1] = rr[around(AWAY[k])] + near[k, 0] + near[k, 1]
+        send(16, agg.at[k - 1], far.at[k], {"fsdp": around(AWAY[k])})
+
+    arrived(4, near.at[pl.ds(3, 2)])
+    forward(3)
+    forward(4)
+    arrived(15, near.at[pl.ds(0, 3)])
+    forward(1)
+    forward(2)
     pass_gram(gy, gx, 6)
 
     arrived(5, d_recv.at[pl.ds(0, 7)])
@@ -245,13 +266,15 @@
     qt1 = dots(split(first_inverse, 3), split(qt, 3), NN, 3)
     share_gram(qt1, hy, hx, 8)
 
-    arrived(4, rr_recv.at[pl.ds(0, 15)])
-    total = rr_recv[0]
-    for k in range(1, 16):
-        total = total + rr_recv[k]
+    total = rr[z] + near[0, 0] + near[0, 1]
+    arrived(16, far)
+    for k in range(5):
+        total = total + far[k]
     rr_all[z] = total
-    for o, peer in column:
-        send(11, rr_all.at[z], rr_all.at[z], peer)
+    for k in (3, 4, 1, 2):
+        send(16 + k, rr_all.at[z], rr_all.at[z], {"fsdp": around(AWAY[k])})
+    for step in (8, 1, -1):
+        send(11, rr_all.at[z], rr_all.at[z], {"fsdp": around(step)})
 
     arrived(10, sd_recv.at[pl.ds(0, 15)])
     total = sd_recv[0]
@@ -261,24 +284,45 @@
     for o, peer in column:
         send(12, s_sub.at[z], s_sub.at[z], peer)
 
+    def hand_on(k):
+        o = around(-AWAY[k])
+        arrived(16 + k, rr_all.at[o])
+        for step in (1, -1):
+            send(11, rr_all.at[o], rr_all.at[o], {"fsdp": around(step)})
+
     pass_gram(hy, hx, 8)
+    hand_on(1)
+    hand_on(2)
+    hand_on(3)
+    hand_on(4)
     g = whole_gram(hx, 8)
     aug[...] = jnp.where(lanes < 64, g, aug[...])
     eliminate(aug)
     inverse = split(aug[:, 64:], 3)
+
+    arrived(12, s_sub.at[pl.ds(0, 15)])
+    for k in range(16):
+        s_all[dp, 4 * k : 4 * k + 4, :] = s_sub[k]
+    for o, peer in replicas:
+        send(13, s_all.at[dp], s_all.at[dp], peer)
+    shared = dots(inverse, split(s_all[dp], 3), NN, 3)
+    sums = jnp.sum(shared * shared, axis=1, keepdims=True)
+    small = lax.broadcasted_iota(jnp.int32, (8, 128), 1)
+    tile = jnp.zeros((8, 128), f32)
+    for i in range(8):
+        tile = jnp.where(small == i, jnp.broadcast_to(sums[8 * i : 8 * i + 8], (8, 128)), tile)
+    spot = core * 16 + q
+    sq[spot] = tile
+    for peer in everyone:
+        send(14, sq.at[spot], sq.at[spot], peer)
+
     leftt = dots(inverse, ptp, NN, 3)
     lp = split(leftt, 2)
     l0 = lp[0].astype(f32)
     l1 = lp[1].astype(f32)
     left3 = jnp.concatenate([l0, l0, l1], axis=0).T.astype(bf16)
 
-    arrived(12, s_sub.at[pl.ds(0, 15)])
-    for k in range(16):
-        s_all[dp, 4 * k : 4 * k + 4, :] = s_sub[k]
-    for o, peer in replicas:
-        send(13, s_all.at[dp], s_all.at[dp], peer)
-
-    arrived(11, rr_all.at[pl.ds(0, 15)])
+    arrived(11, rr_all.at[pl.ds(0, 11)])
     for c in range(4):
         cols = slice(256 * c, 256 * c + 256)
         raw = jnp.concatenate(
@@ -294,21 +338,12 @@
     nm_out.start()
 
     arrived(13, s_all.at[pl.ds(0, 7)])
-    sums = None
     for k in range(8):
-        shared = dots(inverse, split(s_all[k], 3), NN, 3)
-        nr_v[:, 128 * k : 128 * k + 128] = shared
-        sums = shared * shared if sums is None else sums + shared * shared
-    sums = jnp.sum(sums, axis=1, keepdims=True)
-    small = lax.broadcasted_iota(jnp.int32, (8, 128), 1)
-    tile = jnp.zeros((8, 128), f32)
-    for i in range(8):
-        tile = jnp.where(small == i, jnp.broadcast_to(sums[8 * i : 8 * i + 8], (8, 128)), tile)
-    sq[x] = tile
-    for o, peer in xs:
-        send(14, sq.at[x], sq.at[x], peer)
-    arrived(14, sq.at[pl.ds(0, 3)])
-    tile = (sq[0] + sq[1]) + (sq[2] + sq[3])
+        nr_v[:, 128 * k : 128 * k + 128] = dots(inverse, split(s_all[k], 3), NN, 3)
+    arrived(14, sq.at[pl.ds(0, 31)])
+    tile = sq[0]
+    for k in range(1, 32):
+        tile = tile + sq[k]
     tile = 1.0 / jnp.sqrt(tile + epsilon)
     factor = jnp.concatenate([lane_of(tile, i) for i in range(8)], axis=0)
     for k in range(8):
@@ -330,34 +365,52 @@
     sent(1, p_send.at[pl.ds(0, 15)])
     sent(2, pk.at[pl.ds(0, 15)])
     sent(3, qk.at[pl.ds(0, 15)])
-    sent(4, rr.at[pl.ds(0, 15)])
+    sent(4, rr.at[pl.ds(0, 4)])
+    sent(15, rr.at[pl.ds(0, 6)])
+    sent(16, far)
+    for k in range(1, 5):
+        sent(16 + k, rr_all.at[0])
     sent(5, d_recv.at[pl.ds(0, 7)])
     sent(6, gy.at[pl.ds(0, 3)])
     sent(7, gx.at[pl.ds(0, 3)])
     sent(8, hy.at[pl.ds(0, 3)])
     sent(9, hx.at[pl.ds(0, 3)])
     sent(10, sd.at[pl.ds(0, 15)])
-    sent(11, rr_all.at[pl.ds(0, 15)])
+    sent(11, rr_all.at[pl.ds(0, 11)])
     sent(12, s_sub.at[pl.ds(0, 15)])
     sent(13, s_all.at[pl.ds(0, 7)])
-    sent(14, sq.at[pl.ds(0, 3)])
+    sent(14, sq.at[pl.ds(0, 31)])
     nm_out.wait()
     nr_out.wait()
     nw_out.wait()
+
+
+def place(a, b, c, x, y, z, u, v, w, isem, osem):
+    there = [(a, u, x), (b, v, y), (c, w, z)]
+    reads = [pltpu.make_async_copy(s, m, isem.at[k]) for k, (s, m, t) in enumerate(there)]
+    writes = [pltpu.make_async_copy(m, t, osem.at[k]) for k, (s, m, t) in enumerate(there)]
+    for k in (2, 1, 0):
+        reads[k].start()
+    for k in (2, 1, 0):
+        reads[k].wait()
+        writes[k].start()
+    for k in (2, 1, 0):
+        writes[k].wait()
 
 
 def local(weight, momentum, grads, right_factor):
     rows, cols = weight.shape
     rank = right_factor.shape[0]
     vm = pltpu.VMEM
-    return pl.pallas_call(
+    results = (
+        jax.ShapeDtypeStruct(weight.shape, f32),
+        jax.ShapeDtypeStruct(momentum.shape, bf16),
+        jax.ShapeDtypeStruct(right_factor.shape, f32),
+    )
+    made = pl.pallas_call(
         kernel,
-        out_shape=(
-            jax.ShapeDtypeStruct(weight.shape, f32),
-            jax.ShapeDtypeStruct(momentum.shape, bf16),
-            jax.ShapeDtypeStruct(right_factor.shape, f32),
-        ),
-        in_specs=[pl.BlockSpec(memory_space=pl.ANY)] * 4,
+        out_shape=results,
+        in_specs=[pl.BlockSpec(memory_space=pltpu.HBM)] * 4,
         out_specs=[pl.BlockSpec(memory_space=pl.ANY)] * 3,
         scratch_shapes=[
             vm((rows, cols), f32),
@@ -373,7 +426,9 @@
             vm((16, 8, 128), f32),
             vm((16, 8, 128), f32),
             vm((16, 32, 128), f32),
-            vm((16, 32, 128), f32),
+            vm((5, 2, 32, 128), f32),
+            vm((4, 32, 128), f32),
+            vm((5, 32, 128), f32),
             vm((16, 32, 128), f32),
             vm((8, 2, 32, 128), f32),
             vm((16, 4, 128), f32),
@@ -385,20 +440,29 @@
             vm((4, 32, 128), f32),
             vm((4, 32, 128), f32),
             vm((64, 128), f32),
-            vm((4, 8, 128), f32),
+            vm((32, 8, 128), f32),
             vm((rows, cols), f32),
             vm((rows, cols), bf16),
             vm((rank, cols), f32),
             pltpu.SemaphoreType.DMA((4,)),
             pltpu.SemaphoreType.DMA((3,)),
-            pltpu.SemaphoreType.DMA((15,)),
-            pltpu.SemaphoreType.DMA((15,)),
+            pltpu.SemaphoreType.DMA((21,)),
+            pltpu.SemaphoreType.DMA((21,)),
         ],
         compiler_params=pltpu.CompilerParams(
-            collective_id=0, has_side_effects=True, vmem_limit_bytes=48 * 1024 * 1024
+            collective_id=0, has_side_effects=True, vmem_limit_bytes=63 * 1024 * 1024
         ),
         name="dion_step",
     )(weight, momentum, grads, right_factor)
+    return pl.pallas_call(
+        place,
+        out_shape=results,
+        in_specs=[pl.BlockSpec(memory_space=pl.ANY)] * 3,
+        out_specs=[pl.BlockSpec(memory_space=pl.ANY)] * 3,
+        scratch_shapes=[vm(r.shape, r.dtype) for r in results]
+        + [pltpu.SemaphoreType.DMA((3,)), pltpu.SemaphoreType.DMA((3,))],
+        name="place",
+    )(*made)
 
 
 def solution(mesh):

time: 76.3 us -> 64.5 us (0.85)
  local copies, waits for them, and re-layouts: 6.9 us -> 0 us
  Pallas kernels: 68.5 us -> 63.6 us
    unnamed x11 -> x0, local copies, waits for them, and re-layouts: 6.9 us -> none
    pallas_call x1 -> x2, Pallas kernels: 68.5 us -> 63.6 us  [the longest x1 61.1 us: local(): pl.pallas_call(kernel, out_shape=results, in_specs=[pl.BlockSpec(memory_s...]
where the time goes in v2:
time: 64.5 us; the launch traced here: 64.3 us
  Pallas kernels  63.6 us (99%)
    pallas_call x1, Pallas kernels, local(): pl.pallas_call(kernel, out_shape=results, in_specs=[pl.BlockSpec(memory_s...  61.1 us
    pallas_call x1, Pallas kernels, local(): pl.pallas_call(place, out_shape=results, in_specs=[pl.BlockSpec(memory_sp...  2.49 us

profile of v2, /device:TPU:1, one launch (start us, length us, event | category | flops | bytes accessed | tf_op | source)
XLA Modules:
  0.0 64.3 jit_solution(11272280576999707573)
XLA Ops:
  0.6 61.1 %dion_step.1 = (f32[256,1024]{1,0:T(8,128)}, bf16[1,256,1024]{2,1,0:T(8,128)(2,1)}, f32[64,1024]{1,0:T(8,128)}) custom-call(f32[256,1024]{1,0:T(8,128)} %w_hbm.1, bf16[1,256,1024]{2,1,0:T(8,128)(2,1)} %m_hbm.1, bf16[1,2,256,1024]{3,2,1,0:T(8,128)(2,1)} %g_hbm.1, f32[64,1024]{1,0:T(8,128)} %r_hbm.1), custom_call_target="tpu_custom_call" | custom-call | tf_op jit(solution)/shard_map/dion_step/pallas_call | solution.py:410
  61.8 2.5 %place.1 = (f32[256,1024]{1,0:T(8,128)}, bf16[1,256,1024]{2,1,0:T(8,128)(2,1)}, f32[64,1024]{1,0:T(8,128)}) custom-call(f32[256,1024]{1,0:T(8,128)} %get-tuple-element.6.a, bf16[1,256,1024]{2,1,0:T(8,128)(2,1)} %get-tuple-element.7.b, f32[64,1024]{1,0:T(8,128)} %get-tuple-element.8.c), custom_call_target="tpu_custom_call" | custom-call | tf_op jit(solution)/shard_map/place/pallas_call | solution.py:457

commit v3 on v2

--- a/solution.py
+++ b/solution.py
@@ -89,13 +89,13 @@
 
 
 def kernel(
-    w_hbm, m_hbm, g_hbm, r_hbm, nw_hbm, nm_hbm, nr_hbm,
-    w_v, m_v, g_v, r_v, bhi, blo,
-    pc_send, pc_recv, p_send, p_recv, pk, qk,
+    m_hbm, g_hbm, r_hbm, left_hbm, nm_hbm, nr_hbm,
+    m_v, g_v, r_v, bhi, blo,
+    p_send, p_recv, pk, qk,
     rr, near, agg, far, rr_all, d_recv, sd, sd_recv, s_sub, s_all,
     gy, gx, hy, hx, aug, sq,
-    nw_v, nm_v, nr_v,
-    in_sem, out_sem, ssem, rsem,
+    left_v, nm_v, nr_v,
+    in_sem, out_sem, ssem, rsem, beyond,
 ):
     dp = lax.axis_index("dp")
     z = lax.axis_index("fsdp")
@@ -108,7 +108,6 @@
         pltpu.make_async_copy(m_hbm.at[0], m_v, in_sem.at[0]),
         pltpu.make_async_copy(g_hbm.at[0], g_v, in_sem.at[1]),
         pltpu.make_async_copy(r_hbm, r_v, in_sem.at[2]),
-        pltpu.make_async_copy(w_hbm, w_v, in_sem.at[3]),
     ]
     for load in loads:
         load.start()
@@ -116,11 +115,10 @@
     def around(k):
         return lax.rem(z + k + 16, 16)
 
-    mate = {"dp": y * 2 + 1 - core}
-    across = [mate]
-    for d in range(1, 16):
+    across = []
+    for d in range(16):
         o = lax.rem(q + d, 16)
-        across.append({"dp": (o // 4) * 2 + 1 - core, "tensor": lax.rem(o, 4)})
+        across.append((o, {"dp": (o // 4) * 2 + 1 - core, "tensor": lax.rem(o, 4)}))
     plane = []
     for d in range(1, 16):
         o = lax.rem(q + d, 16)
@@ -141,8 +139,8 @@
         xs.append((o, {"tensor": o}))
 
     barrier = pltpu.get_barrier_semaphore()
-    everyone = [p for _, p in plane] + across
-    greeted = [p for _, p in column] + everyone
+    everyone = plane + across
+    greeted = [p for _, p in everyone] + [{"fsdp": around(k)} for d in range(1, 5) for k in (d, -d)]
     for p in greeted:
         pl.semaphore_signal(barrier, inc=1, device_id=p, device_id_type=MESH)
 
@@ -170,19 +168,20 @@
         bhi[rows, :] = bp[0]
         blo[rows, :] = bp[1]
         halves.append(dots(bp, rp, NT, 2) * 0.125)
-    pc_send[...] = jnp.concatenate(halves, axis=1)
+    p_send[...] = jnp.concatenate(halves, axis=1).reshape(16, 8, 128)
 
     pl.semaphore_wait(barrier, len(greeted))
-
-    send(0, pc_send, pc_recv, mate)
-    arrived(0, pc_recv)
-    p_send[...] = (pc_send[...] + pc_recv[...]).reshape(16, 8, 128)
-    p_recv[q] = p_send[q]
-    for o, peer in plane:
-        send(1, p_send.at[o], p_recv.at[q], peer)
-    arrived(1, p_recv.at[pl.ds(0, 15)])
+    for k in (4, -4):
+        pl.semaphore_signal(beyond, inc=1, device_id={"fsdp": around(k)}, device_id_type=MESH)
+
+    spot = core * 16 + q
+    for o, peer in everyone:
+        send(1, p_send.at[o], p_recv.at[spot], peer)
+    p_recv[spot] = p_send[q]
+    pl.semaphore_wait(beyond, 2)
+    arrived(1, p_recv.at[pl.ds(0, 31)])
     mine = p_recv[0]
-    for k in range(1, 16):
+    for k in range(1, 32):
         mine = mine + p_recv[k]
     pk[q] = mine
     qk[z] = mine
@@ -311,9 +310,8 @@
     tile = jnp.zeros((8, 128), f32)
     for i in range(8):
         tile = jnp.where(small == i, jnp.broadcast_to(sums[8 * i : 8 * i + 8], (8, 128)), tile)
-    spot = core * 16 + q
     sq[spot] = tile
-    for peer in everyone:
+    for _, peer in everyone:
         send(14, sq.at[spot], sq.at[spot], peer)
 
     leftt = dots(inverse, ptp, NN, 3)
@@ -321,6 +319,9 @@
     l0 = lp[0].astype(f32)
     l1 = lp[1].astype(f32)
     left3 = jnp.concatenate([l0, l0, l1], axis=0).T.astype(bf16)
+    left_v[...] = left3
+    left_out = pltpu.make_async_copy(left_v, left_hbm, out_sem.at[2])
+    left_out.start()
 
     arrived(11, rr_all.at[pl.ds(0, 11)])
     for c in range(4):
@@ -350,19 +351,8 @@
         nr_v[:, 128 * k : 128 * k + 128] = nr_v[:, 128 * k : 128 * k + 128] * factor
     nr_out = pltpu.make_async_copy(nr_v, nr_hbm, out_sem.at[1])
     nr_out.start()
-    loads[3].wait()
-    scale = learn_rate * math.sqrt(ROWS / COLS)
-    for c in range(4):
-        cols = slice(256 * c, 256 * c + 256)
-        r0, r1 = split(nr_v[:, cols], 2)
-        right3 = jnp.concatenate([r0, r1, r0], axis=0)
-        step = lax.dot_general(left3, right3, NN, preferred_element_type=f32)
-        nw_v[:, cols] = w_v[:, cols] - scale * step
-    nw_out = pltpu.make_async_copy(nw_v, nw_hbm, out_sem.at[2])
-    nw_out.start()
-
-    sent(0, pc_send)
-    sent(1, p_send.at[pl.ds(0, 15)])
+
+    sent(1, p_recv.at[pl.ds(0, 31)])
     sent(2, pk.at[pl.ds(0, 15)])
     sent(3, qk.at[pl.ds(0, 15)])
     sent(4, rr.at[pl.ds(0, 4)])
@@ -382,47 +372,63 @@
     sent(14, sq.at[pl.ds(0, 31)])
     nm_out.wait()
     nr_out.wait()
-    nw_out.wait()
-
-
-def place(a, b, c, x, y, z, u, v, w, isem, osem):
-    there = [(a, u, x), (b, v, y), (c, w, z)]
-    reads = [pltpu.make_async_copy(s, m, isem.at[k]) for k, (s, m, t) in enumerate(there)]
-    writes = [pltpu.make_async_copy(m, t, osem.at[k]) for k, (s, m, t) in enumerate(there)]
-    for k in (2, 1, 0):
-        reads[k].start()
-    for k in (2, 1, 0):
-        reads[k].wait()
-        writes[k].start()
-    for k in (2, 1, 0):
-        writes[k].wait()
+    left_out.wait()
+
+
+def finish(
+    w_hbm, left_hbm, nm_in, nr_in, nw_out, nm_out, nr_out,
+    w_v, left_v, nm_v, nr_v, isem, osem,
+):
+    rows = w_v.shape[1]
+    parts = range(w_v.shape[0])
+    reads = [
+        pltpu.make_async_copy(nr_in, nr_v, isem.at[0]),
+        pltpu.make_async_copy(left_hbm, left_v, isem.at[1]),
+    ]
+    reads += [pltpu.make_async_copy(w_hbm.at[pl.ds(rows * k, rows)], w_v.at[k], isem.at[3 + k]) for k in parts]
+    reads.append(pltpu.make_async_copy(nm_in, nm_v, isem.at[2]))
+    for read in reads:
+        read.start()
+    reads[0].wait()
+    writes = [pltpu.make_async_copy(nr_v, nr_out, osem.at[0])]
+    writes[0].start()
+    scale = learn_rate * math.sqrt(ROWS / COLS)
+    r0, r1 = split(nr_v[...], 2)
+    right3 = jnp.concatenate([r0, r1, r0], axis=0)
+    reads[1].wait()
+    for k in parts:
+        reads[2 + k].wait()
+        step = lax.dot_general(left_v[rows * k : rows * k + rows], right3, NN, preferred_element_type=f32)
+        w_v[k] = w_v[k] - scale * step
+        writes.append(pltpu.make_async_copy(w_v.at[k], nw_out.at[pl.ds(rows * k, rows)], osem.at[2 + k]))
+        writes[-1].start()
+    reads[-1].wait()
+    writes.append(pltpu.make_async_copy(nm_v, nm_out, osem.at[1]))
+    writes[-1].start()
+    for write in writes:
+        write.wait()
 
 
 def local(weight, momentum, grads, right_factor):
     rows, cols = weight.shape
     rank = right_factor.shape[0]
     vm = pltpu.VMEM
-    results = (
-        jax.ShapeDtypeStruct(weight.shape, f32),
-        jax.ShapeDtypeStruct(momentum.shape, bf16),
-        jax.ShapeDtypeStruct(right_factor.shape, f32),
-    )
-    made = pl.pallas_call(
+    new_weight = jax.ShapeDtypeStruct(weight.shape, f32)
+    new_momentum = jax.ShapeDtypeStruct(momentum.shape, bf16)
+    new_right = jax.ShapeDtypeStruct(right_factor.shape, f32)
+    left, made_momentum, made_right = pl.pallas_call(
         kernel,
-        out_shape=results,
-        in_specs=[pl.BlockSpec(memory_space=pltpu.HBM)] * 4,
+        out_shape=(jax.ShapeDtypeStruct((rows, 3 * rank), bf16), new_momentum, new_right),
+        in_specs=[pl.BlockSpec(memory_space=pltpu.HBM)] * 3,
         out_specs=[pl.BlockSpec(memory_space=pl.ANY)] * 3,
         scratch_shapes=[
-            vm((rows, cols), f32),
             vm((rows, cols), bf16),
             vm((2, rows, cols), bf16),
             vm((rank, cols), f32),
             vm((rows, cols), bf16),
             vm((rows, cols), bf16),
-            vm((128, 128), f32),
-            vm((128, 128), f32),
             vm((16, 8, 128), f32),
-            vm((16, 8, 128), f32),
+            vm((32, 8, 128), f32),
             vm((16, 8, 128), f32),
             vm((16, 8, 128), f32),
             vm((16, 32, 128), f32),
@@ -441,28 +447,37 @@
             vm((4, 32, 128), f32),
             vm((64, 128), f32),
             vm((32, 8, 128), f32),
-            vm((rows, cols), f32),
+            vm((rows, 3 * rank), bf16),
             vm((rows, cols), bf16),
             vm((rank, cols), f32),
-            pltpu.SemaphoreType.DMA((4,)),
+            pltpu.SemaphoreType.DMA((3,)),
             pltpu.SemaphoreType.DMA((3,)),
             pltpu.SemaphoreType.DMA((21,)),
             pltpu.SemaphoreType.DMA((21,)),
+            pltpu.SemaphoreType.REGULAR,
         ],
         compiler_params=pltpu.CompilerParams(
             collective_id=0, has_side_effects=True, vmem_limit_bytes=63 * 1024 * 1024
         ),
         name="dion_step",
-    )(weight, momentum, grads, right_factor)
+    )(momentum, grads, right_factor)
+    parts = 4
     return pl.pallas_call(
-        place,
-        out_shape=results,
-        in_specs=[pl.BlockSpec(memory_space=pl.ANY)] * 3,
+        finish,
+        out_shape=(new_weight, new_momentum, new_right),
+        in_specs=[pl.BlockSpec(memory_space=pl.ANY)] * 4,
         out_specs=[pl.BlockSpec(memory_space=pl.ANY)] * 3,
-        scratch_shapes=[vm(r.shape, r.dtype) for r in results]
-        + [pltpu.SemaphoreType.DMA((3,)), pltpu.SemaphoreType.DMA((3,))],
+        scratch_shapes=[
+            vm((parts, rows // parts, cols), f32),
+            vm((rows, 3 * rank), bf16),
+            vm((1, rows, cols), bf16),
+            vm((rank, cols), f32),
+            pltpu.SemaphoreType.DMA((3 + parts,)),
+            pltpu.SemaphoreType.DMA((2 + parts,)),
+        ],
+        compiler_params=pltpu.CompilerParams(vmem_limit_bytes=63 * 1024 * 1024),
         name="place",
-    )(*made)
+    )(weight, left, made_momentum, made_right)
 
 
 def solution(mesh):

time: 64.5 us -> 60.1 us (0.932)
  Pallas kernels: 63.6 us -> 59.3 us
    pallas_call x2, Pallas kernels: 63.6 us -> 59.3 us  [the longest x1 56.4 us: local(): pl.pallas_call(kernel, out_shape=(jax.ShapeDtypeStruct((rows, 3 * rank),...]
where the time goes in v3:
time: 60.1 us; the launch traced here: 59.9 us
  Pallas kernels  59.3 us (99%)
  between operations  0.64 us (1%)
    pallas_call x1, Pallas kernels, local(): pl.pallas_call(kernel, out_shape=(jax.ShapeDtypeStruct((rows, 3 * rank),...  56.4 us
    pallas_call x1, Pallas kernels, local(): pl.pallas_call(finish, out_shape=(new_weight, new_momentum, new_right), i...  2.86 us

profile of v3, /device:TPU:1, one launch (start us, length us, event | category | flops | bytes accessed | tf_op | source)
XLA Modules:
  0.0 59.9 jit_solution(2883628989413837592)
XLA Ops:
  0.6 56.4 %dion_step.1 = (bf16[256,192]{1,0:T(8,128)(2,1)}, bf16[1,256,1024]{2,1,0:T(8,128)(2,1)}, f32[64,1024]{1,0:T(8,128)}) custom-call(bf16[1,256,1024]{2,1,0:T(8,128)(2,1)} %m_hbm.1, bf16[1,2,256,1024]{3,2,1,0:T(8,128)(2,1)} %g_hbm.1, f32[64,1024]{1,0:T(8,128)} %r_hbm.1), custom_call_target="tpu_custom_call" | custom-call | tf_op jit(solution)/shard_map/dion_step/pallas_call | solution.py:419
  57.1 2.9 %place.1 = (f32[256,1024]{1,0:T(8,128)}, bf16[1,256,1024]{2,1,0:T(8,128)(2,1)}, f32[64,1024]{1,0:T(8,128)}) custom-call(f32[256,1024]{1,0:T(8,128)} %w_hbm.1, bf16[256,192]{1,0:T(8,128)(2,1)} %get-tuple-element.6.left_hbm, bf16[1,256,1024]{2,1,0:T(8,128)(2,1)} %get-tuple-element.7.nm_in, f32[64,1024]{1,0:T(8,128)} %get-tuple-element.8.nr_in), custom_call_target="tpu_custom_call" | custom-call | tf_op jit(solution)/shard_map/place/pallas_call | solution.py:465

commit v4 on v3

--- a/solution.py
+++ b/solution.py
@@ -53,45 +53,40 @@
 
 def eliminate(ref):
     sub = lax.broadcasted_iota(jnp.int32, (8, 128), 0)
-
-    def body(kb, _):
-        o = pl.multiple_of(kb * 8, 8)
-        shift = lax.rem(128 - 8 * kb, 128)
-        R = ref[pl.ds(o, 8), :]
-        W = [R] + [ref[8 * i : 8 * i + 8, :] for i in range(1, 8)]
-        D = [pltpu.roll(w, shift, 1) for w in W]
-        C = [[lane_of(d, j) for j in range(8)] for d in D]
-        Ls = [[None] * 8 for _ in range(8)]
+    W = [ref[8 * i : 8 * i + 8, :] for i in range(8)]
+    for kb in range(8):
+        C = [[lane_of(w, 8 * kb + j) for j in range(8)] for w in W]
+        Ls = [[None] * 8 for _ in W]
+        R = W[0]
         us = []
         for j in range(8):
             r = lax.rsqrt(row_of(C[0][j], j))
-            for i in range(8):
+            for i in range(len(W)):
                 Ls[i][j] = C[i][j] * r
             u = row_of(R, j) * r
             us.append(u)
             R = R - Ls[0][j] * u
             for k in range(j + 1, 8):
                 s = row_of(Ls[0][j], k)
-                for i in range(8):
+                for i in range(len(W)):
                     C[i][k] = C[i][k] - Ls[i][j] * s
         U = us[0]
         for j in range(1, 8):
             U = jnp.where(sub == j, us[j], U)
-        for i in range(1, 8):
+        ref[8 * kb : 8 * kb + 8, :] = U
+        rest = []
+        for i in range(1, len(W)):
             w = W[i]
             for j in range(8):
                 w = w - Ls[i][j] * us[j]
-            ref[8 * i : 8 * i + 8, :] = jnp.where(i > kb, w, W[i])
-        ref[pl.ds(o, 8), :] = U
-        return 0
-
-    lax.fori_loop(0, 8, body, 0)
+            rest.append(w)
+        W = rest
 
 
 def kernel(
     m_hbm, g_hbm, r_hbm, left_hbm, nm_hbm, nr_hbm,
     m_v, g_v, r_v, bhi, blo,
-    p_send, p_recv, pk, qk,
+    p_send, p_recv, px, pk, qk,
     rr, near, agg, far, rr_all, d_recv, sd, sd_recv, s_sub, s_all,
     gy, gx, hy, hx, aug, sq,
     left_v, nm_v, nr_v,
@@ -101,8 +96,27 @@
     z = lax.axis_index("fsdp")
     x = lax.axis_index("tensor")
     y = dp // 2
-    core = lax.rem(dp, 2)
+    core = lax.bitwise_and(dp, 1)
     q = y * 4 + x
+
+    def around(k):
+        return lax.bitwise_and(z + (k + 16), 15)
+
+    replicas = []
+    for d in (4, 5, 2, 3, 6, 7, 1):
+        o = lax.bitwise_xor(dp, d)
+        replicas.append((o, {"dp": o}))
+    ys, xs = [], []
+    for d in (2, 1, 3):
+        o = lax.bitwise_xor(y, d)
+        ys.append((o, {"dp": o * 2 + core}))
+        o = lax.bitwise_xor(x, d)
+        xs.append((o, {"tensor": o}))
+
+    barrier = pltpu.get_barrier_semaphore()
+    greeted = [p for _, p in replicas] + [p for _, p in xs] + [{"fsdp": around(k)} for k in (2, -2, 1, -1)]
+    for p in greeted:
+        pl.semaphore_signal(barrier, inc=1, device_id=p, device_id_type=MESH)
 
     loads = [
         pltpu.make_async_copy(m_hbm.at[0], m_v, in_sem.at[0]),
@@ -112,37 +126,9 @@
     for load in loads:
         load.start()
 
-    def around(k):
-        return lax.rem(z + k + 16, 16)
-
-    across = []
-    for d in range(16):
-        o = lax.rem(q + d, 16)
-        across.append((o, {"dp": (o // 4) * 2 + 1 - core, "tensor": lax.rem(o, 4)}))
-    plane = []
-    for d in range(1, 16):
-        o = lax.rem(q + d, 16)
-        plane.append((o, {"dp": (o // 4) * 2 + core, "tensor": lax.rem(o, 4)}))
-    column = []
-    for d in range(1, 16):
-        o = lax.rem(z + d, 16)
-        column.append((o, {"fsdp": o}))
-    replicas = []
-    for d in range(1, 8):
-        o = lax.rem(dp + d, 8)
-        replicas.append((o, {"dp": o}))
-    ys, xs = [], []
-    for d in range(1, 4):
-        o = lax.rem(y + d, 4)
-        ys.append((o, {"dp": o * 2 + core}))
-        o = lax.rem(x + d, 4)
-        xs.append((o, {"tensor": o}))
-
-    barrier = pltpu.get_barrier_semaphore()
-    everyone = plane + across
-    greeted = [p for _, p in everyone] + [{"fsdp": around(k)} for d in range(1, 5) for k in (d, -d)]
-    for p in greeted:
-        pl.semaphore_signal(barrier, inc=1, device_id=p, device_id_type=MESH)
+    def tell(level, step):
+        for k in (step, -step):
+            pl.semaphore_signal(beyond.at[level], inc=1, device_id={"fsdp": around(k)}, device_id_type=MESH)
 
     def send(phase, src, dst, peer):
         pltpu.make_async_remote_copy(
@@ -168,29 +154,37 @@
         bhi[rows, :] = bp[0]
         blo[rows, :] = bp[1]
         halves.append(dots(bp, rp, NT, 2) * 0.125)
-    p_send[...] = jnp.concatenate(halves, axis=1).reshape(16, 8, 128)
+    p_send[...] = jnp.concatenate(halves, axis=1).reshape(4, 32, 128)
 
     pl.semaphore_wait(barrier, len(greeted))
-    for k in (4, -4):
-        pl.semaphore_signal(beyond, inc=1, device_id={"fsdp": around(k)}, device_id_type=MESH)
-
-    spot = core * 16 + q
-    for o, peer in everyone:
-        send(1, p_send.at[o], p_recv.at[spot], peer)
-    p_recv[spot] = p_send[q]
-    pl.semaphore_wait(beyond, 2)
-    arrived(1, p_recv.at[pl.ds(0, 31)])
+    tell(0, 2)
+
+    for o, peer in replicas:
+        send(0, p_send.at[o // 2], p_recv.at[dp], peer)
+    p_recv[dp] = p_send[y]
+    pl.semaphore_wait(beyond.at[0], 2)
+    tell(1, 4)
+    arrived(0, p_recv.at[pl.ds(0, 7)])
     mine = p_recv[0]
-    for k in range(1, 32):
+    for k in range(1, 8):
         mine = mine + p_recv[k]
-    pk[q] = mine
-    qk[z] = mine
-    for o, peer in plane:
-        send(2, pk.at[q], pk.at[q], peer)
+    px[x] = mine
+    for o, peer in xs:
+        send(1, px.at[x], px.at[x], peer)
+    pl.semaphore_wait(beyond.at[1], 2)
+    arrived(1, px.at[pl.ds(0, 3)])
+    pk[y] = (px[0] + px[1]) + (px[2] + px[3])
+    for o, peer in ys:
+        send(2, pk.at[y], pk.at[y], peer)
+    qk[z] = pk[y, pl.ds(pl.multiple_of(8 * x, 8), 8)]
+    column = []
+    for d in (8, 7, 9, 6, 10, 5, 11, 4, 12, 3, 13, 2, 14, 1, 15):
+        o = around(d)
+        column.append((o, {"fsdp": o}))
     for o, peer in column:
         send(3, qk.at[z], qk.at[z], peer)
 
-    arrived(2, pk.at[pl.ds(0, 15)])
+    arrived(2, pk.at[pl.ds(0, 3)])
     pt = pk[...].reshape(128, 128).T
     pt = jnp.concatenate([pt[:64], pt[64:]], axis=1)
     ptp = split(pt, 3)
@@ -200,13 +194,13 @@
         for k in range(2):
             for h in range(2):
                 rr[4 * c + 2 * k + h] = part[32 * h : 32 * h + 32, 128 * k : 128 * k + 128]
+    for o, peer in replicas:
+        send(5, rr.at[pl.ds(2 * o, 2)], d_recv.at[dp], peer)
     for k in (3, 4, 1, 2, 0):
         for side, step in enumerate((1, -1)):
             o = around(step + AWAY[k])
             send(4 if k > 2 else 15, rr.at[o], near.at[k, side], {"fsdp": around(step)})
     send(16, rr.at[around(8)], far.at[0], {"fsdp": around(8)})
-    for o, peer in replicas:
-        send(5, rr.at[pl.ds(2 * o, 2)], d_recv.at[dp], peer)
     d_recv[dp] = rr[pl.ds(2 * dp, 2)]
 
     def share_gram(t, first, second, phase):
@@ -239,12 +233,6 @@
         agg[k - 1] = rr[around(AWAY[k])] + near[k, 0] + near[k, 1]
         send(16, agg.at[k - 1], far.at[k], {"fsdp": around(AWAY[k])})
 
-    arrived(4, near.at[pl.ds(3, 2)])
-    forward(3)
-    forward(4)
-    arrived(15, near.at[pl.ds(0, 3)])
-    forward(1)
-    forward(2)
     pass_gram(gy, gx, 6)
 
     arrived(5, d_recv.at[pl.ds(0, 7)])
@@ -257,6 +245,12 @@
     for o, peer in column:
         send(10, sd.at[o], sd_recv.at[z], peer)
     sd_recv[z] = sd[z]
+    arrived(4, near.at[pl.ds(3, 2)])
+    forward(3)
+    forward(4)
+    arrived(15, near.at[pl.ds(0, 3)])
+    forward(1)
+    forward(2)
 
     g = whole_gram(gx, 6)
     aug[...] = jnp.where(lanes < 64, g, jnp.where(lanes == ranks + 64, 1.0, 0.0))
@@ -264,6 +258,14 @@
     first_inverse = aug[:, 64:]
     qt1 = dots(split(first_inverse, 3), split(qt, 3), NN, 3)
     share_gram(qt1, hy, hx, 8)
+
+    arrived(10, sd_recv.at[pl.ds(0, 15)])
+    total = sd_recv[0]
+    for k in range(1, 16):
+        total = total + sd_recv[k]
+    s_sub[z] = total * 0.125
+    for o, peer in column:
+        send(12, s_sub.at[z], s_sub.at[z], peer)
 
     total = rr[z] + near[0, 0] + near[0, 1]
     arrived(16, far)
@@ -275,14 +277,6 @@
     for step in (8, 1, -1):
         send(11, rr_all.at[z], rr_all.at[z], {"fsdp": around(step)})
 
-    arrived(10, sd_recv.at[pl.ds(0, 15)])
-    total = sd_recv[0]
-    for k in range(1, 16):
-        total = total + sd_recv[k]
-    s_sub[z] = total * 0.125
-    for o, peer in column:
-        send(12, s_sub.at[z], s_sub.at[z], peer)
-
     def hand_on(k):
         o = around(-AWAY[k])
         arrived(16 + k, rr_all.at[o])
@@ -292,8 +286,6 @@
     pass_gram(hy, hx, 8)
     hand_on(1)
     hand_on(2)
-    hand_on(3)
-    hand_on(4)
     g = whole_gram(hx, 8)
     aug[...] = jnp.where(lanes < 64, g, aug[...])
     eliminate(aug)
@@ -310,10 +302,19 @@
     tile = jnp.zeros((8, 128), f32)
     for i in range(8):
         tile = jnp.where(small == i, jnp.broadcast_to(sums[8 * i : 8 * i + 8], (8, 128)), tile)
+    spot = core * 16 + q
     sq[spot] = tile
-    for _, peer in everyone:
+    everyone = []
+    for d in (10, 9, 11, 6, 14, 2, 8, 5, 7, 13, 15, 1, 3, 4, 12, 0):
+        o = lax.bitwise_xor(q, d)
+        everyone.append({"dp": (o // 4) * 2 + 1 - core, "tensor": lax.bitwise_and(o, 3)})
+        if d > 0:
+            everyone.append({"dp": (o // 4) * 2 + core, "tensor": lax.bitwise_and(o, 3)})
+    for peer in everyone:
         send(14, sq.at[spot], sq.at[spot], peer)
 
+    hand_on(3)
+    hand_on(4)
     leftt = dots(inverse, ptp, NN, 3)
     lp = split(leftt, 2)
     l0 = lp[0].astype(f32)
@@ -352,8 +353,9 @@
     nr_out = pltpu.make_async_copy(nr_v, nr_hbm, out_sem.at[1])
     nr_out.start()
 
-    sent(1, p_recv.at[pl.ds(0, 31)])
-    sent(2, pk.at[pl.ds(0, 15)])
+    sent(0, p_recv.at[pl.ds(0, 7)])
+    sent(1, px.at[pl.ds(0, 3)])
+    sent(2, pk.at[pl.ds(0, 3)])
     sent(3, qk.at[pl.ds(0, 15)])
     sent(4, rr.at[pl.ds(0, 4)])
     sent(15, rr.at[pl.ds(0, 6)])
@@ -427,9 +429,10 @@
             vm((rank, cols), f32),
             vm((rows, cols), bf16),
             vm((rows, cols), bf16),
-            vm((16, 8, 128), f32),
-            vm((32, 8, 128), f32),
-            vm((16, 8, 128), f32),
+            vm((4, 32, 128), f32),
+            vm((8, 32, 128), f32),
+            vm((4, 32, 128), f32),
+            vm((4, 32, 128), f32),
             vm((16, 8, 128), f32),
             vm((16, 32, 128), f32),
             vm((5, 2, 32, 128), f32),
@@ -454,7 +457,7 @@
             pltpu.SemaphoreType.DMA((3,)),
             pltpu.SemaphoreType.DMA((21,)),
             pltpu.SemaphoreType.DMA((21,)),
-            pltpu.SemaphoreType.REGULAR,
+            pltpu.SemaphoreType.REGULAR((2,)),
         ],
         compiler_params=pltpu.CompilerParams(
             collective_id=0, has_side_effects=True, vmem_limit_bytes=63 * 1024 * 1024

time: 60.1 us -> 58 us (0.965)
  Pallas kernels: 59.3 us -> 57.2 us
    pallas_call x1, Pallas kernels: 56.4 us -> 54.3 us  [local(): pl.pallas_call(kernel, out_shape=(jax.ShapeDtypeStruct((rows, 3 * rank),...]
where the time goes in v4:
time: 58 us; the launch traced here: 57.8 us
  Pallas kernels  57.2 us (99%)
  between operations  0.64 us (1%)
    pallas_call x1, Pallas kernels, local(): pl.pallas_call(kernel, out_shape=(jax.ShapeDtypeStruct((rows, 3 * rank),...  54.3 us
    pallas_call x1, Pallas kernels, local(): pl.pallas_call(finish, out_shape=(new_weight, new_momentum, new_right), i...  2.86 us

profile of v4, /device:TPU:1, one launch (start us, length us, event | category | flops | bytes accessed | tf_op | source)
XLA Modules:
  0.0 57.8 jit_solution(12724489652359793624)
XLA Ops:
  0.6 54.3 %dion_step.1 = (bf16[256,192]{1,0:T(8,128)(2,1)}, bf16[1,256,1024]{2,1,0:T(8,128)(2,1)}, f32[64,1024]{1,0:T(8,128)}) custom-call(bf16[1,256,1024]{2,1,0:T(8,128)(2,1)} %m_hbm.1, bf16[1,2,256,1024]{3,2,1,0:T(8,128)(2,1)} %g_hbm.1, f32[64,1024]{1,0:T(8,128)} %r_hbm.1), custom_call_target="tpu_custom_call" | custom-call | tf_op jit(solution)/shard_map/dion_step/pallas_call | solution.py:421
  55.0 2.9 %place.1 = (f32[256,1024]{1,0:T(8,128)}, bf16[1,256,1024]{2,1,0:T(8,128)(2,1)}, f32[64,1024]{1,0:T(8,128)}) custom-call(f32[256,1024]{1,0:T(8,128)} %w_hbm.1, bf16[256,192]{1,0:T(8,128)(2,1)} %get-tuple-element.6.left_hbm, bf16[1,256,1024]{2,1,0:T(8,128)(2,1)} %get-tuple-element.7.nm_in, f32[64,1024]{1,0:T(8,128)} %get-tuple-element.8.nr_in), custom_call_target="tpu_custom_call" | custom-call | tf_op jit(solution)/shard_map/place/pallas_call | solution.py:468

commit v5 on v4

--- a/solution.py
+++ b/solution.py
@@ -84,12 +84,12 @@
 
 
 def kernel(
-    m_hbm, g_hbm, r_hbm, left_hbm, nm_hbm, nr_hbm,
+    m_hbm, g_hbm, r_hbm, left_hbm, nm_hbm, nr_hbm, norm_hbm,
     m_v, g_v, r_v, bhi, blo,
     p_send, p_recv, px, pk, qk,
     rr, near, agg, far, rr_all, d_recv, sd, sd_recv, s_sub, s_all,
     gy, gx, hy, hx, aug, sq,
-    left_v, nm_v, nr_v,
+    left_v, nm_v, nr_v, norm_v,
     in_sem, out_sem, ssem, rsem, beyond,
 ):
     dp = lax.axis_index("dp")
@@ -284,8 +284,6 @@
             send(11, rr_all.at[o], rr_all.at[o], {"fsdp": around(step)})
 
     pass_gram(hy, hx, 8)
-    hand_on(1)
-    hand_on(2)
     g = whole_gram(hx, 8)
     aug[...] = jnp.where(lanes < 64, g, aug[...])
     eliminate(aug)
@@ -313,8 +311,8 @@
     for peer in everyone:
         send(14, sq.at[spot], sq.at[spot], peer)
 
-    hand_on(3)
-    hand_on(4)
+    for k in range(1, 5):
+        hand_on(k)
     leftt = dots(inverse, ptp, NN, 3)
     lp = split(leftt, 2)
     l0 = lp[0].astype(f32)
@@ -342,16 +340,15 @@
     arrived(13, s_all.at[pl.ds(0, 7)])
     for k in range(8):
         nr_v[:, 128 * k : 128 * k + 128] = dots(inverse, split(s_all[k], 3), NN, 3)
+    nr_out = pltpu.make_async_copy(nr_v, nr_hbm, out_sem.at[1])
+    nr_out.start()
     arrived(14, sq.at[pl.ds(0, 31)])
     tile = sq[0]
     for k in range(1, 32):
         tile = tile + sq[k]
-    tile = 1.0 / jnp.sqrt(tile + epsilon)
-    factor = jnp.concatenate([lane_of(tile, i) for i in range(8)], axis=0)
-    for k in range(8):
-        nr_v[:, 128 * k : 128 * k + 128] = nr_v[:, 128 * k : 128 * k + 128] * factor
-    nr_out = pltpu.make_async_copy(nr_v, nr_hbm, out_sem.at[1])
-    nr_out.start()
+    norm_v[...] = 1.0 / jnp.sqrt(tile + epsilon)
+    norm_out = pltpu.make_async_copy(norm_v, norm_hbm, out_sem.at[3])
+    norm_out.start()
 
     sent(0, p_recv.at[pl.ds(0, 7)])
     sent(1, px.at[pl.ds(0, 3)])
@@ -375,11 +372,12 @@
     nm_out.wait()
     nr_out.wait()
     left_out.wait()
+    norm_out.wait()
 
 
 def finish(
-    w_hbm, left_hbm, nm_in, nr_in, nw_out, nm_out, nr_out,
-    w_v, left_v, nm_v, nr_v, isem, osem,
+    w_hbm, left_hbm, nm_in, nr_in, norm_in, nw_out, nm_out, nr_out,
+    w_v, left_v, nm_v, nr_v, norm_v, isem, osem,
 ):
     rows = w_v.shape[1]
     parts = range(w_v.shape[0])
@@ -389,9 +387,16 @@
     ]
     reads += [pltpu.make_async_copy(w_hbm.at[pl.ds(rows * k, rows)], w_v.at[k], isem.at[3 + k]) for k in parts]
     reads.append(pltpu.make_async_copy(nm_in, nm_v, isem.at[2]))
+    norm = pltpu.make_async_copy(norm_in, norm_v, isem.at[3 + len(parts)])
+    norm.start()
     for read in reads:
         read.start()
+    norm.wait()
+    tile = norm_v[...]
+    factor = jnp.concatenate([lane_of(tile, i) for i in range(8)], axis=0)
     reads[0].wait()
+    for k in range(nr_v.shape[1] // 128):
+        nr_v[:, 128 * k : 128 * k + 128] = nr_v[:, 128 * k : 128 * k + 128] * factor
     writes = [pltpu.make_async_copy(nr_v, nr_out, osem.at[0])]
     writes[0].start()
     scale = learn_rate * math.sqrt(ROWS / COLS)
@@ -418,11 +423,11 @@
     new_weight = jax.ShapeDtypeStruct(weight.shape, f32)
     new_momentum = jax.ShapeDtypeStruct(momentum.shape, bf16)
     new_right = jax.ShapeDtypeStruct(right_factor.shape, f32)
-    left, made_momentum, made_right = pl.pallas_call(
+    left, made_momentum, made_right, norm = pl.pallas_call(
         kernel,
-        out_shape=(jax.ShapeDtypeStruct((rows, 3 * rank), bf16), new_momentum, new_right),
+        out_shape=(jax.ShapeDtypeStruct((rows, 3 * rank), bf16), new_momentum, new_right, jax.ShapeDtypeStruct((8, 128), f32)),
         in_specs=[pl.BlockSpec(memory_space=pltpu.HBM)] * 3,
-        out_specs=[pl.BlockSpec(memory_space=pl.ANY)] * 3,
+        out_specs=[pl.BlockSpec(memory_space=pl.ANY)] * 4,
         scratch_shapes=[
             vm((rows, cols), bf16),
             vm((2, rows, cols), bf16),
@@ -453,8 +458,9 @@
             vm((rows, 3 * rank), bf16),
             vm((rows, cols), bf16),
             vm((rank, cols), f32),
+            vm((8, 128), f32),
             pltpu.SemaphoreType.DMA((3,)),
-            pltpu.SemaphoreType.DMA((3,)),
+            pltpu.SemaphoreType.DMA((4,)),
             pltpu.SemaphoreType.DMA((21,)),
             pltpu.SemaphoreType.DMA((21,)),
             pltpu.SemaphoreType.REGULAR((2,)),
@@ -468,19 +474,20 @@
     return pl.pallas_call(
         finish,
         out_shape=(new_weight, new_momentum, new_right),
-        in_specs=[pl.BlockSpec(memory_space=pl.ANY)] * 4,
+        in_specs=[pl.BlockSpec(memory_space=pl.ANY)] * 5,
         out_specs=[pl.BlockSpec(memory_space=pl.ANY)] * 3,
         scratch_shapes=[
             vm((parts, rows // parts, cols), f32),
             vm((rows, 3 * rank), bf16),
             vm((1, rows, cols), bf16),
             vm((rank, cols), f32),
-            pltpu.SemaphoreType.DMA((3 + parts,)),
+            vm((8, 128), f32),
+            pltpu.SemaphoreType.DMA((4 + parts,)),
             pltpu.SemaphoreType.DMA((2 + parts,)),
         ],
         compiler_params=pltpu.CompilerParams(vmem_limit_bytes=63 * 1024 * 1024),
         name="place",
-    )(weight, left, made_momentum, made_right)
+    )(weight, left, made_momentum, made_right, norm)
 
 
 def solution(mesh):

time: 58 us -> 57.9 us (level)
  no operation moved by 1% of the time
where the time goes in v5:
time: 57.9 us; the launch traced here: 57.7 us
  Pallas kernels  57.1 us (99%)
  between operations  0.64 us (1%)
    pallas_call x1, Pallas kernels, local(): pl.pallas_call(kernel, out_shape=(jax.ShapeDtypeStruct((rows, 3 * rank),...  54.2 us
    pallas_call x1, Pallas kernels, local(): pl.pallas_call(finish, out_shape=(new_weight, new_momentum, new_right), i...  2.87 us

profile of v5, /device:TPU:1, one launch (start us, length us, event | category | flops | bytes accessed | tf_op | source)
XLA Modules:
  0.0 57.7 jit_solution(16361549163210447035)
XLA Ops:
  0.6 54.2 %dion_step.1 = (bf16[256,192]{1,0:T(8,128)(2,1)}, bf16[1,256,1024]{2,1,0:T(8,128)(2,1)}, f32[64,1024]{1,0:T(8,128)}, f32[8,128]{1,0:T(8,128)}) custom-call(bf16[1,256,1024]{2,1,0:T(8,128)(2,1)} %m_hbm.1, bf16[1,2,256,1024]{3,2,1,0:T(8,128)(2,1)} %g_hbm.1, f32[64,1024]{1,0:T(8,128)} %r_hbm.1), custom_call_target="tpu_custom_call" | custom-call | tf_op jit(solution)/shard_map/dion_step/pallas_call | solution.py:426
  54.8 2.9 %place.1 = (f32[256,1024]{1,0:T(8,128)}, bf16[1,256,1024]{2,1,0:T(8,128)(2,1)}, f32[64,1024]{1,0:T(8,128)}) custom-call(f32[256,1024]{1,0:T(8,128)} %w_hbm.1, bf16[256,192]{1,0:T(8,128)(2,1)} %get-tuple-element.7.left_hbm, bf16[1,256,1024]{2,1,0:T(8,128)(2,1)} %get-tuple-element.8.nm_in, f32[64,1024]{1,0:T(8,128)} %get-tuple-element.9.nr_in, ...), custom_call_target="tpu_custom_call" | custom-call | tf_op jit(solution)/shard_map/place/pallas_call | solution.py:474

commit v6 on v5

--- a/solution.py
+++ b/solution.py
@@ -203,9 +203,9 @@
     send(16, rr.at[around(8)], far.at[0], {"fsdp": around(8)})
     d_recv[dp] = rr[pl.ds(2 * dp, 2)]
 
-    def share_gram(t, first, second, phase):
-        tp = split(t, 3)
-        g = dots(tp, tp, NT, 3)
+    def share_gram(t, first, second, phase, order):
+        tp = split(t, order)
+        g = dots(tp, tp, NT, order)
         first[y] = jnp.concatenate([g[:32], g[32:]], axis=1)
         for o, peer in ys:
             send(phase, first.at[y], first.at[y], peer)
@@ -227,7 +227,7 @@
     arrived(3, qk.at[pl.ds(0, 15)])
     qt = qk[...].reshape(128, 128).T
     qt = jnp.concatenate([qt[:64], qt[64:]], axis=1)
-    share_gram(qt, gy, gx, 6)
+    share_gram(qt, gy, gx, 6, 3)
 
     def forward(k):
         agg[k - 1] = rr[around(AWAY[k])] + near[k, 0] + near[k, 1]
@@ -257,7 +257,7 @@
     eliminate(aug)
     first_inverse = aug[:, 64:]
     qt1 = dots(split(first_inverse, 3), split(qt, 3), NN, 3)
-    share_gram(qt1, hy, hx, 8)
+    share_gram(qt1, hy, hx, 8, 2)
 
     arrived(10, sd_recv.at[pl.ds(0, 15)])
     total = sd_recv[0]

time: 57.9 us -> 57.8 us (level)
  no operation moved by 1% of the time
where the time goes in v6:
time: 57.8 us; the launch traced here: 57.7 us
  Pallas kernels  57 us (99%)
  between operations  0.64 us (1%)
    pallas_call x1, Pallas kernels, local(): pl.pallas_call(kernel, out_shape=(jax.ShapeDtypeStruct((rows, 3 * rank),...  54.1 us
    pallas_call x1, Pallas kernels, local(): pl.pallas_call(finish, out_shape=(new_weight, new_momentum, new_right), i...  2.87 us

profile of v6, /device:TPU:1, one launch (start us, length us, event | category | flops | bytes accessed | tf_op | source)
XLA Modules:
  0.0 57.7 jit_solution(2761987716354370780)
XLA Ops:
  0.6 54.1 %dion_step.1 = (bf16[256,192]{1,0:T(8,128)(2,1)}, bf16[1,256,1024]{2,1,0:T(8,128)(2,1)}, f32[64,1024]{1,0:T(8,128)}, f32[8,128]{1,0:T(8,128)}) custom-call(bf16[1,256,1024]{2,1,0:T(8,128)(2,1)} %m_hbm.1, bf16[1,2,256,1024]{3,2,1,0:T(8,128)(2,1)} %g_hbm.1, f32[64,1024]{1,0:T(8,128)} %r_hbm.1), custom_call_target="tpu_custom_call" | custom-call | tf_op jit(solution)/shard_map/dion_step/pallas_call | solution.py:426
  54.8 2.9 %place.1 = (f32[256,1024]{1,0:T(8,128)}, bf16[1,256,1024]{2,1,0:T(8,128)(2,1)}, f32[64,1024]{1,0:T(8,128)}) custom-call(f32[256,1024]{1,0:T(8,128)} %w_hbm.1, bf16[256,192]{1,0:T(8,128)(2,1)} %get-tuple-element.7.left_hbm, bf16[1,256,1024]{2,1,0:T(8,128)(2,1)} %get-tuple-element.8.nm_in, f32[64,1024]{1,0:T(8,128)} %get-tuple-element.9.nr_in, ...), custom_call_target="tpu_custom_call" | custom-call | tf_op jit(solution)/shard_map/place/pallas_call | solution.py:474
